TPU v7x, 32 devices: a whole 2x2x4 slice. The times are simulated.
32 devices in a mesh: wide: 16 (over z, y, core), batch: 2 (over x).
Axes of the slice: x: 2, y: 2, z: 4, core: 2. Of those that a mesh axis runs over, the one named last changes fastest.
Arguments:
- integrals: bfloat16 [1536, 16, 640], P('wide'), may hold values from -0.8984375 to 0.8984375
- vir_coeff: bfloat16 [640, 512], P(None, 'batch'), may hold values from -0.25 to 0.25
- occ_energy: float32 [16], replicated, may hold values from -1.6 to -0.4
- vir_energy: float32 [512], replicated, may hold values from 0.2 to 3
- kappas: float32 [8], replicated, may hold values from 0.1 to 3
Outputs:
- density: bfloat16 [8, 16, 512, 1536], P(None, 'wide', 'batch')
All inputs are finite; a program needn't handle non-finite values.
Results may differ from a plain program's by a relative error of at most 0.0051.
Values may be sent and summed in bfloat16 or wider, within the bound.
No kernel may reach another device: no remote copies, remote signals or barrier semaphores. Data moves between devices by JAX's collectives and lax.ppermute only.
A program may use at most 128 MiB of HBM per device.

v0:
```python
import functools

import jax
import jax.numpy as jnp
from jax import lax
from jax.experimental import pallas as pl
from jax.experimental.pallas import tpu as pltpu
from jax.sharding import PartitionSpec as P

HALF = 2
PARTNERS = ("own", "sibling", "third", "near", "far")
VMEM_LIMIT = 18 * 1024 * 1024
LANES = 128


def from_behind(shard, axis, by):
    peers = lax.axis_size(axis)
    return lax.ppermute(shard, axis, [(i, (i + by) % peers) for i in range(peers)])


def swap_by(shard, axis, bit):
    peers = lax.axis_size(axis)
    return lax.ppermute(shard, axis, [(i, i ^ bit) for i in range(peers)])


def hand_along(shard, axis):
    peers = lax.axis_size(axis)
    return lax.ppermute(
        shard,
        axis,
        [(i, (i + (4 if i // 2 % 2 == 0 else -4)) % peers) for i in range(peers)],
    )


def cut_kernel(own, low, high):
    cut = low.shape[1]
    low[...] = own[:, :cut]
    high[...] = own[:, cut:]


def cut_in_two(own):
    vmem = pl.BlockSpec(memory_space=pltpu.VMEM)
    half = jax.ShapeDtypeStruct((own.shape[0], own.shape[1] // 2), own.dtype)
    return pl.pallas_call(
        cut_kernel,
        out_shape=(half, half),
        in_specs=[vmem],
        out_specs=(vmem, vmem),
        compiler_params=pltpu.CompilerParams(vmem_limit_bytes=VMEM_LIMIT),
        cost_estimate=pl.CostEstimate(flops=1, bytes_accessed=1, transcendentals=0),
    )(own)


def make_tables(place, energies, vir_rows, own_low, own_high, made):
    own_t, row_energies, row_factors, column_energies, column_factors = made
    nkap, rows = row_factors.shape[0], own_t.shape[0]
    orbital, half, count = place[0], place[1], place[2]
    core_sign = 1 - 2 * lax.rem(orbital, 2)
    pair_sign = 1 - 2 * lax.rem(lax.div(orbital, 2), 2)
    offsets = dict(
        own=0, sibling=core_sign, third=-core_sign, near=HALF * pair_sign, far=-HALF * pair_sign
    )

    def down_columns(row):
        return jnp.transpose(jnp.broadcast_to(row, (LANES, rows)))

    own_t[:rows // 2, :] = jnp.transpose(own_low[...])
    own_t[rows // 2:, :] = jnp.transpose(own_high[...])
    row_energy = vir_rows[pl.ds(half, 1), :] - energies[nkap + orbital]
    row_energies[...] = down_columns(row_energy)
    for q in range(nkap):
        row_factors[q] = down_columns(jnp.exp(-energies[q] * row_energy))
    for row, name in enumerate(PARTNERS):
        index = lax.rem(orbital + offsets[name] + count, count)
        for other in range(2):
            energy = vir_rows[pl.ds(lax.rem(half + other, 2), 1), :] - energies[nkap + index]
            at = slice(2 * row + other, 2 * row + other + 1)
            column_energies[at, :] = energy
            for q in range(nkap):
                column_factors[q, at, :] = jnp.exp(-energies[q] * energy)


def terms_kernel(pieces, mode, shape, *refs):
    if mode == "first":
        place, energies, vir_rows = refs[:3]
        partners = refs[3:3 + len(pieces)]
        *made, out, amp, ratio = refs[3 + len(pieces):]
        make_tables(place, energies, vir_rows, partners[0], partners[1], made)
    else:
        made = refs[:5]
        partners = refs[5:5 + len(pieces)]
        partial, *refs = refs[5 + len(pieces):]
        if mode == "last":
            result, amp, ratio, out, sems = refs
        else:
            out, amp, ratio = refs
    own_t, row_energies, row_factors, column_energies, column_factors = made
    group_size, p_tile = shape
    nkap, rows = row_factors.shape[0], row_factors.shape[1]
    naux = own_t.shape[1]

    columns_at = []
    for (name, other, start), partner in zip(pieces, partners):
        row = 2 * PARTNERS.index(name) + other
        for c in range(start, start + partner.shape[1], LANES):
            columns_at.append((slice(row, row + 1), slice(c, c + LANES)))
    width = LANES * len(columns_at)

    def partner_columns(tile):
        return jnp.concatenate([partner[tile, :] for partner in partners], axis=1)

    for at in range(0, width, 2 * LANES):
        columns = partner_columns(slice(None))[:, at:at + 2 * LANES]
        coulomb = jnp.dot(own_t[...], columns, preferred_element_type=jnp.float32)
        for c in range(0, columns.shape[1], LANES):
            ratio[:, at + c:at + c + LANES] = -coulomb[:, c:c + LANES] / (
                row_energies[...] + column_energies[columns_at[(at + c) // LANES]]
            )

    copies = []
    for group in range(0, nkap, group_size):
        top, bottom = group * rows, (group + group_size) * rows
        for q in range(group, group + group_size):
            for position, (row, lanes) in enumerate(columns_at):
                columns = slice(position * LANES, (position + 1) * LANES)
                damping = 1.0 - row_factors[q] * column_factors[q, row, lanes]
                amp[q * rows:(q + 1) * rows, columns] = (
                    ratio[:, columns] * damping * damping
                ).astype(amp.dtype)
        span = slice(group, group + group_size)
        for start in range(0, naux, p_tile):
            tile = slice(start, start + p_tile)
            value = lax.dot_general(
                amp[top:bottom, :],
                partner_columns(tile),
                (((1,), (1,)), ((), ())),
                preferred_element_type=jnp.float32,
            ).reshape(group_size, rows, p_tile)
            if mode != "first":
                value = value + partial[span, :, tile]
            out[span, :, tile] = value.astype(out.dtype)
            if mode == "last":
                copy = pltpu.make_async_copy(
                    out.at[span, :, tile], result.at[span, 0, :, tile], sems.at[len(copies)]
                )
                copy.start()
                copies.append(copy)
    for copy in copies:
        copy.wait()


def add_terms(place, energies, vir_rows, nkap, made, partners, partial, shape, last=False):
    pieces = tuple(partner[:3] for partner in partners)
    arrays = [partner[3] for partner in partners]
    naux = arrays[0].shape[0]
    rows = vir_rows.shape[1]
    width = sum(array.shape[1] for array in arrays)
    vmem = pl.BlockSpec(memory_space=pltpu.VMEM)
    smem = pl.BlockSpec(memory_space=pltpu.SMEM)
    density = jax.ShapeDtypeStruct((nkap, rows, naux), jnp.float32)
    scratch = [
        pltpu.VMEM((nkap * rows, width), jnp.bfloat16),
        pltpu.VMEM((rows, width), jnp.float32),
    ]
    aliases = {}
    if made is None:
        mode = "first"
        operands = [place, energies, vir_rows] + arrays
        in_specs = [smem, smem] + [vmem] * (1 + len(arrays))
        out_shape = (
            jax.ShapeDtypeStruct((rows, naux), arrays[0].dtype),
            jax.ShapeDtypeStruct((rows, LANES), jnp.float32),
            jax.ShapeDtypeStruct((nkap, rows, LANES), jnp.float32),
            jax.ShapeDtypeStruct((2 * len(PARTNERS), rows), jnp.float32),
            jax.ShapeDtypeStruct((nkap, 2 * len(PARTNERS), rows), jnp.float32),
            density,
        )
        out_specs = (vmem,) * 6
    else:
        mode = "last" if last else "middle"
        operands = list(made) + arrays + [partial]
        in_specs = [vmem] * len(operands)
        if last:
            out_shape = jax.ShapeDtypeStruct((nkap, 1, rows, naux), jnp.bfloat16)
            out_specs = pl.BlockSpec(memory_space=pl.ANY)
            scratch.append(pltpu.VMEM((nkap, rows, naux), jnp.bfloat16))
            scratch.append(pltpu.SemaphoreType.DMA((nkap // shape[0] * (naux // shape[1]),)))
        else:
            out_shape, out_specs = density, vmem
            aliases = {len(operands) - 1: 0}
    return pl.pallas_call(
        functools.partial(terms_kernel, pieces, mode, shape),
        out_shape=out_shape,
        input_output_aliases=aliases,
        in_specs=in_specs,
        out_specs=out_specs,
        scratch_shapes=scratch,
        compiler_params=pltpu.CompilerParams(vmem_limit_bytes=VMEM_LIMIT),
        cost_estimate=pl.CostEstimate(flops=1, bytes_accessed=1, transcendentals=0),
    )(*operands)


def pair_terms(integrals, vir_coeff, occ_energy, vir_energy, kappas):
    aux_local, occ_count, basis = integrals.shape
    vir_local = vir_coeff.shape[1]
    wide_index = lax.axis_index("wide")
    batch_index = lax.axis_index("batch")
    place = jnp.stack(
        [wide_index, batch_index, jnp.full((), occ_count, wide_index.dtype)]
    ).astype(jnp.int32)
    vir_rows = vir_energy.reshape(-1, vir_local)
    def to_owner(columns):
        return lax.all_to_all(columns, "wide", split_axis=1, concat_axis=0, tiled=True)[:, 0, :]

    def over_batch(value):
        return from_behind(value, "batch", 1)

    def over_cores(value):
        return swap_by(value, "wide", 1)

    def over_pairs(value):
        return swap_by(value, "wide", 2)

    def along(value):
        return hand_along(value, "wide")

    together = lax.optimization_barrier
    sends_near = ((wide_index ^ (wide_index >> 1)) & 1) == 0
    energies = jnp.concatenate([kappas, occ_energy])
    flat_ints = integrals.reshape(aux_local * occ_count, basis)
    transformed = jnp.dot(flat_ints, vir_coeff, preferred_element_type=jnp.float32).astype(
        jnp.bfloat16
    )
    own, sends_near, vir_rows, place, energies = together(
        (
            to_owner(transformed.reshape(aux_local, occ_count, vir_local)),
            sends_near,
            vir_rows,
            place,
            energies,
        )
    )

    def for_sibling(near, far):
        return over_cores(
            jnp.concatenate([jnp.where(sends_near, *pair) for pair in zip(near, far)], axis=1)
        )

    cut = vir_local // 2
    sibling = over_cores(own)
    low, high = cut_in_two(own)
    step = functools.partial(add_terms, place, energies, vir_rows, kappas.shape[0])

    own_o_high = over_batch(high)
    near_low = over_pairs(low)
    *made, density = step(None, [("own", 0, 0, low), ("own", 0, cut, high)], None, (8, 512))
    step = functools.partial(step, made)

    low, high, density = together((low, high, density))
    own_o_low = over_batch(low)
    near_high = over_pairs(high)
    density = step([("sibling", 0, 0, sibling)], density, (8, 512))

    near_low, own_o_high, density = together((near_low, own_o_high, density))
    near_o_high = over_pairs(own_o_high)
    far_low = along(near_low)
    density = step([("own", 1, cut, own_o_high), ("near", 0, 0, near_low)], density, (8, 512))

    own_o_low, own_o_high, near_low, near_high, density = together(
        (own_o_low, own_o_high, near_low, near_high, density)
    )
    far_high = along(near_high)
    near_o_low = over_batch(near_low)
    sibling_o = over_cores(jnp.concatenate([own_o_low, own_o_high], axis=1))
    density = step([("own", 1, 0, own_o_low), ("near", 0, cut, near_high)], density, (8, 512))

    near_o_high, far_low, density = together((near_o_high, far_low, density))
    far_o_high = along(near_o_high)
    far_o_low = over_batch(far_low)
    density = step([("far", 0, 0, far_low), ("near", 1, cut, near_o_high)], density, (8, 512))

    far_low, far_high, near_o_low, density = together((far_low, far_high, near_o_low, density))
    third_low = for_sibling((near_low,), (far_low,))
    third_high = for_sibling((near_high,), (far_high,))
    density = step(
        [("near", 1, 0, near_o_low), ("far", 0, cut, far_high), ("sibling", 1, 0, sibling_o)],
        density,
        (2, 512),
    )

    far_o_high, far_o_low, density = together((far_o_high, far_o_low, density))
    third_o_low = for_sibling((near_o_low,), (far_o_low,))
    third_o_high = for_sibling((near_o_high,), (far_o_high,))
    return step(
        [
            ("third", 0, 0, third_low),
            ("third", 0, cut, third_high),
            ("far", 1, 0, far_o_low),
            ("far", 1, cut, far_o_high),
            ("third", 1, 0, third_o_low),
            ("third", 1, cut, third_o_high),
        ],
        density,
        (2, 512),
        last=True,
    )


def pair_density(own_slice, partner, own_energy, partner_energy, row_energy, vir_energy, kappas):
    coulomb = lax.dot_general(
        own_slice, partner, (((0,), (0,)), ((), ())), preferred_element_type=jnp.float32
    )
    denominator = row_energy[:, None] + vir_energy[None, :] - own_energy - partner_energy
    damping = 1.0 - jnp.exp(-kappas[:, None, None] * denominator[None])
    amplitude = (-coulomb[None] * (damping * damping) / denominator[None]).astype(jnp.bfloat16)
    flat = amplitude.reshape(-1, amplitude.shape[2])
    density = lax.dot_general(
        flat, partner, (((1,), (1,)), ((), ())), preferred_element_type=jnp.float32
    )
    return density.reshape(kappas.shape[0], own_slice.shape[1], partner.shape[0])


def ring_terms(integrals, vir_coeff, occ_energy, vir_energy, kappas):
    aux_local, occ_count, basis = integrals.shape
    vir_local = vir_coeff.shape[1]
    batch_index = lax.axis_index("batch")
    wide_index = lax.axis_index("wide")
    flat_ints = integrals.reshape(aux_local * occ_count, basis)
    row_energy = lax.dynamic_slice_in_dim(vir_energy, batch_index * vir_local, vir_local, 0)
    own_energy = lax.dynamic_slice_in_dim(occ_energy, wide_index, 1, 0)[0]

    def term(partner, offset, own_slice):
        partner_index = (wide_index + offset) % occ_count
        partner_energy = lax.dynamic_slice_in_dim(occ_energy, partner_index, 1, 0)[0]
        return pair_density(
            own_slice, partner, own_energy, partner_energy, row_energy, vir_energy, kappas
        )

    transformed = jnp.dot(flat_ints, vir_coeff, preferred_element_type=jnp.float32).astype(
        jnp.bfloat16
    )
    transformed = transformed.reshape(aux_local, occ_count, vir_local)
    own_slice = lax.all_to_all(transformed, "wide", split_axis=1, concat_axis=0, tiled=True)[
        :, 0, :
    ]
    own_full = lax.all_gather(own_slice, "batch", axis=1, tiled=True)
    density = term(own_full, 0, own_slice)
    upper = own_full
    lower = own_full
    for offset in range(1, HALF + 1):
        upper = from_behind(upper, "wide", -1)
        lower = from_behind(lower, "wide", 1)
        density = density + term(upper, offset, own_slice) + term(lower, -offset, own_slice)
    return density.astype(jnp.bfloat16)[:, None, :, :]


def solution(mesh):
    paired = mesh.shape["batch"] == 2 and mesh.shape["wide"] % 4 == 0

    return jax.shard_map(
        pair_terms if paired else ring_terms,
        mesh=mesh,
        in_specs=(P("wide", None, None), P(None, "batch"), P(), P(), P()),
        out_specs=P(None, "wide", "batch", None),
        check_vma=False,
    )
```

profile of v0, /device:TPU:1, one launch (start us, length us, event | category | flops | bytes accessed | tf_op | source)
XLA Modules:
  0.0 81.9 jit_solution(5917586700455951193)
XLA Ops:
  0.0 0.0 copy-start
  0.0 1.5 %copy-done = bf16[96,16,640]{2,1,0:T(8,128)(2,1)S(1)} copy-done((bf16[96,16,640]{2,1,0:T(8,128)(2,1)S(1)}, bf16[96,16,640]{2,1,0:T(8,128)(2,1)}, u32[]{:S(2)}) %copy-start) | copy-done | bytes 1966104
  1.5 1.7 %convolution_convert_fusion = bf16[1536,256]{1,0:T(8,128)(2,1)S(1)} fusion(bf16[1536,640]{1,0:T(8,128)(2,1)S(1)} %bitcast.11, bf16[640,256]{1,0:T(8,128)(2,1)} %param.6), kind=kOutput, calls=%fused_computation | convolution fusion | flops 503709696 | bytes 3080192 | tf_op jit(solution)/shard_map/dot_general | solution.py:231
  3.3 0.0 copy-start.1
  3.3 0.0 copy-start.2
  3.3 0.0 copy-start.3
  3.3 1.1 %copy.11 = bf16[96,16,256]{2,0,1:T(8,128)(2,1)} copy(bf16[96,16,256]{2,1,0:T(8,128)(2,1)S(1)} %bitcast.14) | data formatting | bytes 1572864 | tf_op jit(solution)/shard_map/reshape | solution.py:236
  4.5 7.4 %all-to-all-start = ((bf16[96,16,256]{2,0,1:T(8,128)(2,1)}), bf16[96,16,256]{2,0,1:T(8,128)(2,1)S(1)}, u32[]{:S(2)}, u32[]{:S(2)}) async-start(bf16[96,16,256]{2,0,1:T(8,128)(2,1)} %copy.11), calls=%async_computation | async-start | bytes 1572864 | tf_op jit(solution)/shard_map/all_to_all | solution.py:213
  11.8 0.0 copy-done.1
  11.8 0.0 copy-done.2
  11.8 0.0 copy-done.3
  11.9 0.1 pad_maximum_fusion.1.refs_1_
  11.9 0.1 pad_add_fusion.refs_0_
  12.0 18.4 %all-to-all-done = bf16[96,16,256]{2,0,1:T(8,128)(2,1)S(1)} async-done(((bf16[96,16,256]{2,0,1:T(8,128)(2,1)}), bf16[96,16,256]{2,0,1:T(8,128)(2,1)S(1)}, u32[]{:S(2)}, u32[]{:S(2)}) %all-to-all-start) | async-done | bytes 786464 | tf_op jit(solution)/shard_map/all_to_all | solution.py:213
  30.4 0.3 collective-permute-start.3
  30.6 0.1 shard_map.55
  30.8 1.1 %collective-permute-start.1 = (bf16[1536,128]{1,0:T(8,128)(2,1)S(1)}, bf16[1536,128]{1,0:T(8,128)(2,1)S(1)}, u32[]{:S(2)}, u32[]{:S(2)}) collective-permute-start(bf16[1536,128]{1,0:T(8,128)(2,1)S(1)} %get-tuple-element.52.refs_3_), channel_id=1, source_target_pairs={{0,4},{2,6},{4,0},{6,2},{8,12},{10,14},{12,8},{14,10},{16,20},{18,... | collective-permute-start | bytes 1179656 | tf_op jit(solution)/shard_map/ppermute | solution.py:23
  31.9 1.2 %collective-permute-start.2 = (bf16[1536,128]{1,0:T(8,128)(2,1)S(1)}, bf16[1536,128]{1,0:T(8,128)(2,1)S(1)}, u32[]{:S(2)}, u32[]{:S(2)}) collective-permute-start(bf16[1536,128]{1,0:T(8,128)(2,1)S(1)} %get-tuple-element.56.refs_4_), channel_id=1, source_target_pairs={{0,1},{1,0},{2,3},{3,2},{4,5},{5,4},{6,7},{7,6},{8,9},{9,8},{10,11... | collective-permute-start | bytes 1179656 | tf_op jit(solution)/shard_map/ppermute | solution.py:18
  33.1 3.3 %shard_map.56 = (bf16[256,1536]{1,0:T(8,128)(2,1)S(1)}, f32[256,128]{1,0:T(8,128)S(1)}, f32[8,256,128]{2,1,0:T(8,128)S(1)}, f32[10,256]{1,0:T(8,128)S(1)}, f32[8...) custom-call(s32[3]{0:T(128)S(1)} %pad_add_fusion.refs_0_, f32[24]{0:T(128)S(1)} %pad_maximum_fusion.1.refs_1_, ...), custom_call_target="tpu_custom_call" | custom-call | flops 1 | bytes 1 | tf_op jit(solution)/shard_map/pallas_call | solution.py:191
  36.5 0.3 collective-permute-start
  36.8 0.4 collective-permute-start.4
  37.2 0.0 collective-permute-done.3.refs_5_
  37.2 3.0 %shard_map.57.refs_7_ = f32[8,256,1536]{2,1,0:T(8,128)S(1)} custom-call(bf16[256,1536]{1,0:T(8,128)(2,1)S(1)} %get-tuple-element.45.refs_0_, f32[256,128]{1,0:T(8,128)S(1)} %get-tuple-element.46.refs_1_, f32[8,256,128]{2,1,0:T(8,128)S(1)} %get-tuple-element.47.refs_2_, f32[10,256]{1,0:T(8,128)S(1)} %get-tuple-element.48.refs_3_, ...), custom_call_target="tpu_custom_call", output_to_operand_aliasing={{}: (6, {})} | custom-call | flops 1 | bytes 1 | tf_op jit(solution)/shard_map/pallas_call | solution.py:191
  40.2 1.1 %collective-permute-done.1.refs_6_ = bf16[1536,128]{1,0:T(8,128)(2,1)S(1)} collective-permute-done((bf16[1536,128]{1,0:T(8,128)(2,1)S(1)}, bf16[1536,128]{1,0:T(8,128)(2,1)S(1)}, u32[]{:S(2)}, u32[]{:S(2)}) %collective-permute-start.1) | collective-permute-done | bytes 393248 | tf_op jit(solution)/shard_map/ppermute | solution.py:23
  41.3 0.5 collective-permute-done.2.refs_5_
  41.8 0.7 collective-permute-start.5
  42.4 2.0 %collective-permute-start.6 = (bf16[1536,128]{1,0:T(8,128)(2,1)S(1)}, bf16[1536,128]{1,0:T(8,128)(2,1)S(1)}, u32[]{:S(2)}, u32[]{:S(2)}) collective-permute-start(bf16[1536,128]{1,0:T(8,128)(2,1)S(1)} %collective-permute-done.1.refs_6_), channel_id=1, source_target_pairs={{0,8},{2,10},{4,28},{6,30},{8,16},{10,18},{12,4},{14,6},{16,24},{1... | collective-permute-start | bytes 1179656 | tf_op jit(solution)/shard_map/ppermute | solution.py:28
  44.5 3.0 %shard_map.58.refs_7_ = f32[8,256,1536]{2,1,0:T(8,128)S(1)} custom-call(bf16[256,1536]{1,0:T(8,128)(2,1)S(1)} %get-tuple-element.45.refs_0_, f32[256,128]{1,0:T(8,128)S(1)} %get-tuple-element.46.refs_1_, f32[8,256,128]{2,1,0:T(8,128)S(1)} %get-tuple-element.47.refs_2_, f32[10,256]{1,0:T(8,128)S(1)} %get-tuple-element.48.refs_3_, ...), custom_call_target="tpu_custom_call", output_to_operand_aliasing={{}: (7, {})} | custom-call | flops 1 | bytes 1 | tf_op jit(solution)/shard_map/pallas_call | solution.py:191
  47.5 2.7 %collective-permute-done.refs_5_ = bf16[1536,128]{1,0:T(8,128)(2,1)S(1)} collective-permute-done((bf16[1536,128]{1,0:T(8,128)(2,1)S(1)}, bf16[1536,128]{1,0:T(8,128)(2,1)S(1)}, u32[]{:S(2)}, u32[]{:S(2)}) %collective-permute-start) | collective-permute-done | bytes 393248 | tf_op jit(solution)/shard_map/ppermute | solution.py:18
  50.2 0.0 collective-permute-done.4.refs_6_
  50.2 2.4 %collective-permute-start.7 = (bf16[1536,128]{1,0:T(8,128)(2,1)S(1)}, bf16[1536,128]{1,0:T(8,128)(2,1)S(1)}, u32[]{:S(2)}, u32[]{:S(2)}) collective-permute-start(bf16[1536,128]{1,0:T(8,128)(2,1)S(1)} %collective-permute-done.4.refs_6_), channel_id=1, source_target_pairs={{0,8},{2,10},{4,28},{6,30},{8,16},{10,18},{12,4},{14,6},{16,24},{1... | collective-permute-start | bytes 1179656 | tf_op jit(solution)/shard_map/ppermute | solution.py:28
  52.6 1.2 %collective-permute-start.8 = (bf16[1536,128]{1,0:T(8,128)(2,1)S(1)}, bf16[1536,128]{1,0:T(8,128)(2,1)S(1)}, u32[]{:S(2)}, u32[]{:S(2)}) collective-permute-start(bf16[1536,128]{1,0:T(8,128)(2,1)S(1)} %collective-permute-done.1.refs_6_), channel_id=1, source_target_pairs={{0,1},{1,0},{2,3},{3,2},{4,5},{5,4},{6,7},{7,6},{8,9},{9,8},{10,11... | collective-permute-start | bytes 1179656 | tf_op jit(solution)/shard_map/ppermute | solution.py:18
  53.8 0.1 pad_maximum_fusion
  53.9 2.1 %collective-permute-start.13 = (bf16[1536,256]{1,0:T(8,128)(2,1)S(1)}, bf16[1536,256]{1,0:T(8,128)(2,1)S(1)}, u32[]{:S(2)}, u32[]{:S(2)}) collective-permute-start(bf16[1536,256]{1,0:T(8,128)(2,1)S(1)} %pad_maximum_fusion), channel_id=1, source_target_pairs={{0,2},{2,0},{4,6},{6,4},{8,10},{10,8},{12,14},{14,12},{16,18},{18,... | collective-permute-start | bytes 2359304 | tf_op jit(solution)/shard_map/ppermute | solution.py:23
  55.9 3.0 %shard_map.59.refs_7_ = f32[8,256,1536]{2,1,0:T(8,128)S(1)} custom-call(bf16[256,1536]{1,0:T(8,128)(2,1)S(1)} %get-tuple-element.45.refs_0_, f32[256,128]{1,0:T(8,128)S(1)} %get-tuple-element.46.refs_1_, f32[8,256,128]{2,1,0:T(8,128)S(1)} %get-tuple-element.47.refs_2_, f32[10,256]{1,0:T(8,128)S(1)} %get-tuple-element.48.refs_3_, ...), custom_call_target="tpu_custom_call", output_to_operand_aliasing={{}: (7, {})} | custom-call | flops 1 | bytes 1 | tf_op jit(solution)/shard_map/pallas_call | solution.py:191
  59.0 0.0 collective-permute-done.5.refs_6_
  59.0 0.0 collective-permute-done.6.refs_5_
  59.0 1.0 %collective-permute-start.11 = (bf16[1536,128]{1,0:T(8,128)(2,1)S(1)}, bf16[1536,128]{1,0:T(8,128)(2,1)S(1)}, u32[]{:S(2)}, u32[]{:S(2)}) collective-permute-start(bf16[1536,128]{1,0:T(8,128)(2,1)S(1)} %collective-permute-done.5.refs_6_), channel_id=1, source_target_pairs={{0,8},{2,10},{4,28},{6,30},{8,16},{10,18},{12,4},{14,6},{16,24},{1... | collective-permute-start | bytes 1179656 | tf_op jit(solution)/shard_map/ppermute | solution.py:28
  60.0 1.2 %collective-permute-start.12 = (bf16[1536,128]{1,0:T(8,128)(2,1)S(1)}, bf16[1536,128]{1,0:T(8,128)(2,1)S(1)}, u32[]{:S(2)}, u32[]{:S(2)}) collective-permute-start(bf16[1536,128]{1,0:T(8,128)(2,1)S(1)} %collective-permute-done.6.refs_5_), channel_id=1, source_target_pairs={{0,1},{1,0},{2,3},{3,2},{4,5},{5,4},{6,7},{7,6},{8,9},{9,8},{10,11... | collective-permute-start | bytes 1179656 | tf_op jit(solution)/shard_map/ppermute | solution.py:18
  61.2 3.0 %shard_map.60.refs_8_ = f32[8,256,1536]{2,1,0:T(8,128)S(1)} custom-call(bf16[256,1536]{1,0:T(8,128)(2,1)S(1)} %get-tuple-element.45.refs_0_, f32[256,128]{1,0:T(8,128)S(1)} %get-tuple-element.46.refs_1_, f32[8,256,128]{2,1,0:T(8,128)S(1)} %get-tuple-element.47.refs_2_, f32[10,256]{1,0:T(8,128)S(1)} %get-tuple-element.48.refs_3_, ...), custom_call_target="tpu_custom_call", output_to_operand_aliasing={{}: (7, {})} | custom-call | flops 1 | bytes 1 | tf_op jit(solution)/shard_map/pallas_call | solution.py:191
  64.2 0.0 collective-permute-done.7.refs_6_
  64.2 0.0 collective-permute-done.8.refs_5_
  64.3 2.0 %collective-permute-start.10 = (bf16[1536,128]{1,0:T(8,128)(2,1)S(1)}, bf16[1536,128]{1,0:T(8,128)(2,1)S(1)}, u32[]{:S(2)}, u32[]{:S(2)}) collective-permute-start(bf16[1536,128]{1,0:T(8,128)(2,1)S(1)} %broadcast_select_fusion.2), channel_id=1, source_target_pairs={{0,2},{2,0},{4,6},{6,4},{8,10},{10,8},{12,14},{14,12},{16,18},{18,... | collective-permute-start | bytes 1179656 | tf_op jit(solution)/shard_map/ppermute | solution.py:23
  66.3 0.1 collective-permute-start.9
  66.4 0.0 collective-permute-done.13.refs_7_
  66.4 5.1 %shard_map.61.refs_11_ = f32[8,256,1536]{2,1,0:T(8,128)S(1)} custom-call(bf16[256,1536]{1,0:T(8,128)(2,1)S(1)} %get-tuple-element.45.refs_0_, f32[256,128]{1,0:T(8,128)S(1)} %get-tuple-element.46.refs_1_, f32[8,256,128]{2,1,0:T(8,128)S(1)} %get-tuple-element.47.refs_2_, f32[10,256]{1,0:T(8,128)S(1)} %get-tuple-element.48.refs_3_, ...), custom_call_target="tpu_custom_call", output_to_operand_aliasing={{}: (8, {})} | custom-call | flops 1 | bytes 1 | tf_op jit(solution)/shard_map/pallas_call | solution.py:191
  71.5 0.4 collective-permute-done.11.refs_8_
  71.9 0.0 collective-permute-done.12.refs_7_
  71.9 0.8 collective-permute-start.15
  72.8 0.1 collective-permute-start.14
  72.9 0.0 collective-permute-done.10.refs_6_
  72.9 0.0 collective-permute-done.9.refs_5_
  72.9 1.2 %collective-permute-done.15.refs_10_ = bf16[1536,128]{1,0:T(8,128)(2,1)S(1)} collective-permute-done((bf16[1536,128]{1,0:T(8,128)(2,1)S(1)}, bf16[1536,128]{1,0:T(8,128)(2,1)S(1)}, u32[]{:S(2)}, u32[]{:S(2)}) %collective-permute-start.15) | collective-permute-done | bytes 393248 | tf_op jit(solution)/shard_map/ppermute | solution.py:23
  74.1 0.6 collective-permute-done.14.refs_9_
  74.6 7.1 %shard_map.62 = bf16[8,1,256,1536]{3,2,1,0:T(8,128)(2,1)} custom-call(bf16[256,1536]{1,0:T(8,128)(2,1)S(1)} %get-tuple-element.45.refs_0_, f32[256,128]{1,0:T(8,128)S(1)} %get-tuple-element.46.refs_1_, f32[8,256,128]{2,1,0:T(8,128)S(1)} %get-tuple-element.47.refs_2_, f32[10,256]{1,0:T(8,128)S(1)} %get-tuple-element.48.refs_3_, ...), custom_call_target="tpu_custom_call" | custom-call | flops 1 | bytes 1 | tf_op jit(solution)/shard_map/pallas_call | solution.py:191
  (5 shorter events, 0.2 us)
Async XLA Ops:
  0.0 1.5 %copy-start = (bf16[96,16,640]{2,1,0:T(8,128)(2,1)S(1)}, bf16[96,16,640]{2,1,0:T(8,128)(2,1)}, u32[]{:S(2)}) copy-start(bf16[96,16,640]{2,1,0:T(8,128)(2,1)} %param.5) | copy-start | bytes 5898244
  3.3 8.5 %copy-start.1 = (f32[512]{0:T(512)S(1)}, f32[512]{0:T(512)}, u32[]{:S(2)}) copy-start(f32[512]{0:T(512)} %param.8) | copy-start | bytes 6148
  3.3 8.5 %copy-start.2 = (f32[16]{0:T(128)S(1)}, f32[16]{0:T(128)}, u32[]{:S(2)}) copy-start(f32[16]{0:T(128)} %param.7) | copy-start | bytes 196
  3.3 8.5 %copy-start.3 = (f32[8]{0:T(128)S(1)}, f32[8]{0:T(128)}, u32[]{:S(2)}) copy-start(f32[8]{0:T(128)} %param.9) | copy-start | bytes 100
  4.5 25.9 %all-to-all-start = ((bf16[96,16,256]{2,0,1:T(8,128)(2,1)}), bf16[96,16,256]{2,0,1:T(8,128)(2,1)S(1)}, u32[]{:S(2)}, u32[]{:S(2)}) async-start(bf16[96,16,256]{2,0,1:T(8,128)(2,1)} %copy.11), calls=%async_computation | async-start | bytes 1572864 | tf_op jit(solution)/shard_map/all_to_all | solution.py:213
  30.4 6.8 %collective-permute-start.3 = (bf16[1536,256]{1,0:T(8,128)(2,1)S(1)}, bf16[1536,256]{1,0:T(8,128)(2,1)S(1)}, u32[]{:S(2)}, u32[]{:S(2)}) collective-permute-start(bf16[1536,256]{1,0:T(8,128)(2,1)S(1)} %bitcast.12), channel_id=1, source_target_pairs={{0,2},{2,0},{4,6},{6,4},{8,10},{10,8},{12,14},{14,12},{16,18},{18,... | collective-permute-start | bytes 2359304 | tf_op jit(solution)/shard_map/ppermute | solution.py:23
  30.8 10.5 %collective-permute-start.1 = (bf16[1536,128]{1,0:T(8,128)(2,1)S(1)}, bf16[1536,128]{1,0:T(8,128)(2,1)S(1)}, u32[]{:S(2)}, u32[]{:S(2)}) collective-permute-start(bf16[1536,128]{1,0:T(8,128)(2,1)S(1)} %get-tuple-element.52.refs_3_), channel_id=1, source_target_pairs={{0,4},{2,6},{4,0},{6,2},{8,12},{10,14},{12,8},{14,10},{16,20},{18,... | collective-permute-start | bytes 1179656 | tf_op jit(solution)/shard_map/ppermute | solution.py:23
  31.9 9.9 %collective-permute-start.2 = (bf16[1536,128]{1,0:T(8,128)(2,1)S(1)}, bf16[1536,128]{1,0:T(8,128)(2,1)S(1)}, u32[]{:S(2)}, u32[]{:S(2)}) collective-permute-start(bf16[1536,128]{1,0:T(8,128)(2,1)S(1)} %get-tuple-element.56.refs_4_), channel_id=1, source_target_pairs={{0,1},{1,0},{2,3},{3,2},{4,5},{5,4},{6,7},{7,6},{8,9},{9,8},{10,11... | collective-permute-start | bytes 1179656 | tf_op jit(solution)/shard_map/ppermute | solution.py:18
  36.5 13.7 %collective-permute-start = (bf16[1536,128]{1,0:T(8,128)(2,1)S(1)}, bf16[1536,128]{1,0:T(8,128)(2,1)S(1)}, u32[]{:S(2)}, u32[]{:S(2)}) collective-permute-start(bf16[1536,128]{1,0:T(8,128)(2,1)S(1)} %get-tuple-element.52.refs_3_), channel_id=1, source_target_pairs={{0,1},{1,0},{2,3},{3,2},{4,5},{5,4},{6,7},{7,6},{8,9},{9,8},{10,11... | collective-permute-start | bytes 1179656 | tf_op jit(solution)/shard_map/ppermute | solution.py:18
  36.8 13.4 %collective-permute-start.4 = (bf16[1536,128]{1,0:T(8,128)(2,1)S(1)}, bf16[1536,128]{1,0:T(8,128)(2,1)S(1)}, u32[]{:S(2)}, u32[]{:S(2)}) collective-permute-start(bf16[1536,128]{1,0:T(8,128)(2,1)S(1)} %get-tuple-element.56.refs_4_), channel_id=1, source_target_pairs={{0,4},{2,6},{4,0},{6,2},{8,12},{10,14},{12,8},{14,10},{16,20},{18,... | collective-permute-start | bytes 1179656 | tf_op jit(solution)/shard_map/ppermute | solution.py:23
  41.8 17.2 %collective-permute-start.5 = (bf16[1536,128]{1,0:T(8,128)(2,1)S(1)}, bf16[1536,128]{1,0:T(8,128)(2,1)S(1)}, u32[]{:S(2)}, u32[]{:S(2)}) collective-permute-start(bf16[1536,128]{1,0:T(8,128)(2,1)S(1)} %collective-permute-done.2.refs_5_), channel_id=1, source_target_pairs={{0,4},{2,6},{4,0},{6,2},{8,12},{10,14},{12,8},{14,10},{16,20},{18,... | collective-permute-start | bytes 1179656 | tf_op jit(solution)/shard_map/ppermute | solution.py:23
  42.4 16.5 %collective-permute-start.6 = (bf16[1536,128]{1,0:T(8,128)(2,1)S(1)}, bf16[1536,128]{1,0:T(8,128)(2,1)S(1)}, u32[]{:S(2)}, u32[]{:S(2)}) collective-permute-start(bf16[1536,128]{1,0:T(8,128)(2,1)S(1)} %collective-permute-done.1.refs_6_), channel_id=1, source_target_pairs={{0,8},{2,10},{4,28},{6,30},{8,16},{10,18},{12,4},{14,6},{16,24},{1... | collective-permute-start | bytes 1179656 | tf_op jit(solution)/shard_map/ppermute | solution.py:28
  50.2 14.0 %collective-permute-start.7 = (bf16[1536,128]{1,0:T(8,128)(2,1)S(1)}, bf16[1536,128]{1,0:T(8,128)(2,1)S(1)}, u32[]{:S(2)}, u32[]{:S(2)}) collective-permute-start(bf16[1536,128]{1,0:T(8,128)(2,1)S(1)} %collective-permute-done.4.refs_6_), channel_id=1, source_target_pairs={{0,8},{2,10},{4,28},{6,30},{8,16},{10,18},{12,4},{14,6},{16,24},{1... | collective-permute-start | bytes 1179656 | tf_op jit(solution)/shard_map/ppermute | solution.py:28
  52.6 11.7 %collective-permute-start.8 = (bf16[1536,128]{1,0:T(8,128)(2,1)S(1)}, bf16[1536,128]{1,0:T(8,128)(2,1)S(1)}, u32[]{:S(2)}, u32[]{:S(2)}) collective-permute-start(bf16[1536,128]{1,0:T(8,128)(2,1)S(1)} %collective-permute-done.1.refs_6_), channel_id=1, source_target_pairs={{0,1},{1,0},{2,3},{3,2},{4,5},{5,4},{6,7},{7,6},{8,9},{9,8},{10,11... | collective-permute-start | bytes 1179656 | tf_op jit(solution)/shard_map/ppermute | solution.py:18
  53.9 12.6 %collective-permute-start.13 = (bf16[1536,256]{1,0:T(8,128)(2,1)S(1)}, bf16[1536,256]{1,0:T(8,128)(2,1)S(1)}, u32[]{:S(2)}, u32[]{:S(2)}) collective-permute-start(bf16[1536,256]{1,0:T(8,128)(2,1)S(1)} %pad_maximum_fusion), channel_id=1, source_target_pairs={{0,2},{2,0},{4,6},{6,4},{8,10},{10,8},{12,14},{14,12},{16,18},{18,... | collective-permute-start | bytes 2359304 | tf_op jit(solution)/shard_map/ppermute | solution.py:23
  59.0 12.9 %collective-permute-start.11 = (bf16[1536,128]{1,0:T(8,128)(2,1)S(1)}, bf16[1536,128]{1,0:T(8,128)(2,1)S(1)}, u32[]{:S(2)}, u32[]{:S(2)}) collective-permute-start(bf16[1536,128]{1,0:T(8,128)(2,1)S(1)} %collective-permute-done.5.refs_6_), channel_id=1, source_target_pairs={{0,8},{2,10},{4,28},{6,30},{8,16},{10,18},{12,4},{14,6},{16,24},{1... | collective-permute-start | bytes 1179656 | tf_op jit(solution)/shard_map/ppermute | solution.py:28
  60.0 11.9 %collective-permute-start.12 = (bf16[1536,128]{1,0:T(8,128)(2,1)S(1)}, bf16[1536,128]{1,0:T(8,128)(2,1)S(1)}, u32[]{:S(2)}, u32[]{:S(2)}) collective-permute-start(bf16[1536,128]{1,0:T(8,128)(2,1)S(1)} %collective-permute-done.6.refs_5_), channel_id=1, source_target_pairs={{0,1},{1,0},{2,3},{3,2},{4,5},{5,4},{6,7},{7,6},{8,9},{9,8},{10,11... | collective-permute-start | bytes 1179656 | tf_op jit(solution)/shard_map/ppermute | solution.py:18
  64.3 8.6 %collective-permute-start.10 = (bf16[1536,128]{1,0:T(8,128)(2,1)S(1)}, bf16[1536,128]{1,0:T(8,128)(2,1)S(1)}, u32[]{:S(2)}, u32[]{:S(2)}) collective-permute-start(bf16[1536,128]{1,0:T(8,128)(2,1)S(1)} %broadcast_select_fusion.2), channel_id=1, source_target_pairs={{0,2},{2,0},{4,6},{6,4},{8,10},{10,8},{12,14},{14,12},{16,18},{18,... | collective-permute-start | bytes 1179656 | tf_op jit(solution)/shard_map/ppermute | solution.py:23
  66.3 6.5 %collective-permute-start.9 = (bf16[1536,128]{1,0:T(8,128)(2,1)S(1)}, bf16[1536,128]{1,0:T(8,128)(2,1)S(1)}, u32[]{:S(2)}, u32[]{:S(2)}) collective-permute-start(bf16[1536,128]{1,0:T(8,128)(2,1)S(1)} %broadcast_select_fusion.3), channel_id=1, source_target_pairs={{0,2},{2,0},{4,6},{6,4},{8,10},{10,8},{12,14},{14,12},{16,18},{18,... | collective-permute-start | bytes 1179656 | tf_op jit(solution)/shard_map/ppermute | solution.py:23
  71.9 2.1 %collective-permute-start.15 = (bf16[1536,128]{1,0:T(8,128)(2,1)S(1)}, bf16[1536,128]{1,0:T(8,128)(2,1)S(1)}, u32[]{:S(2)}, u32[]{:S(2)}) collective-permute-start(bf16[1536,128]{1,0:T(8,128)(2,1)S(1)} %broadcast_select_fusion), channel_id=1, source_target_pairs={{0,2},{2,0},{4,6},{6,4},{8,10},{10,8},{12,14},{14,12},{16,18},{18,... | collective-permute-start | bytes 1179656 | tf_op jit(solution)/shard_map/ppermute | solution.py:23
  72.8 1.9 %collective-permute-start.14 = (bf16[1536,128]{1,0:T(8,128)(2,1)S(1)}, bf16[1536,128]{1,0:T(8,128)(2,1)S(1)}, u32[]{:S(2)}, u32[]{:S(2)}) collective-permute-start(bf16[1536,128]{1,0:T(8,128)(2,1)S(1)} %broadcast_select_fusion.1), channel_id=1, source_target_pairs={{0,2},{2,0},{4,6},{6,4},{8,10},{10,8},{12,14},{14,12},{16,18},{18,... | collective-permute-start | bytes 1179656 | tf_op jit(solution)/shard_map/ppermute | solution.py:23
where the time goes:
time: 82.5 us; the launch traced here: 81.9 us
  Pallas kernels  27.8 us (34%)
  waiting for transfers between devices  24.8 us (30%)
  starting transfers between devices  24.2 us (29%)
  local copies, waits for them, and re-layouts  2.7 us (3%)
  matrix products  1.75 us (2%)
    pallas_call x7, Pallas kernels, add_terms(): pl.pallas_call(functools.partial(terms_kernel, pieces, mode, shape), out_...  27.6 us
    all_to_all x1, waiting for transfers between devices, to_owner(): lax.all_to_all(columns, 'wide', split_axis=1, concat_axis=0, tiled=True)  18.4 us
    ppermute x9, starting transfers between devices, swap_by(): return lax.ppermute(shard, axis, [(i, i ^ bit) for i in range(peers)])  7.48 us
    all_to_all x1, starting transfers between devices, to_owner(): lax.all_to_all(columns, 'wide', split_axis=1, concat_axis=0, tiled=True)  7.35 us
    ppermute x3, starting transfers between devices, hand_along(): lax.ppermute(shard, axis, [(i, (i + (4 if i // 2 % 2 == 0 else -4)) % pee...  5.4 us
    ppermute x4, starting transfers between devices, from_behind(): lax.ppermute(shard, axis, [(i, (i + by) % peers) for i in range(peers)])  3.96 us
    ppermute x4, waiting for transfers between devices, from_behind(): lax.ppermute(shard, axis, [(i, (i + by) % peers) for i in range(peers)])  3.18 us
    ppermute x9, waiting for transfers between devices, swap_by(): return lax.ppermute(shard, axis, [(i, i ^ bit) for i in range(peers)])  2.84 us
  transfers between devices with their start and end apart: 17, of which 7 were waited for; matrix products, arithmetic and copies ran while one was open for 1% of the time, Pallas kernels for 25%

commit v1 on v0

--- a/solution.py
+++ b/solution.py
@@ -109,13 +109,14 @@
     def partner_columns(tile):
         return jnp.concatenate([partner[tile, :] for partner in partners], axis=1)
 
-    for at in range(0, width, 2 * LANES):
-        columns = partner_columns(slice(None))[:, at:at + 2 * LANES]
-        coulomb = jnp.dot(own_t[...], columns, preferred_element_type=jnp.float32)
-        for c in range(0, columns.shape[1], LANES):
-            ratio[:, at + c:at + c + LANES] = -coulomb[:, c:c + LANES] / (
-                row_energies[...] + column_energies[columns_at[(at + c) // LANES]]
-            )
+    coulomb = jnp.dot(
+        own_t[...], partner_columns(slice(None)), preferred_element_type=jnp.float32
+    )
+    for position, (row, lanes) in enumerate(columns_at):
+        columns = slice(position * LANES, (position + 1) * LANES)
+        ratio[:, columns] = -coulomb[:, columns] / (
+            row_energies[...] + column_energies[row, lanes]
+        )
 
     copies = []
     for group in range(0, nkap, group_size):
@@ -259,12 +260,12 @@
     low, high, density = together((low, high, density))
     own_o_low = over_batch(low)
     near_high = over_pairs(high)
-    density = step([("sibling", 0, 0, sibling)], density, (8, 512))
+    density = step([("sibling", 0, 0, sibling)], density, (2, 512))
 
     near_low, own_o_high, density = together((near_low, own_o_high, density))
     near_o_high = over_pairs(own_o_high)
     far_low = along(near_low)
-    density = step([("own", 1, cut, own_o_high), ("near", 0, 0, near_low)], density, (8, 512))
+    density = step([("own", 1, cut, own_o_high), ("near", 0, 0, near_low)], density, (2, 1536))
 
     own_o_low, own_o_high, near_low, near_high, density = together(
         (own_o_low, own_o_high, near_low, near_high, density)
@@ -285,7 +286,7 @@
     density = step(
         [("near", 1, 0, near_o_low), ("far", 0, cut, far_high), ("sibling", 1, 0, sibling_o)],
         density,
-        (2, 512),
+        (2, 1536),
     )
 
     far_o_high, far_o_low, density = together((far_o_high, far_o_low, density))
@@ -301,7 +302,7 @@
             ("third", 1, cut, third_o_high),
         ],
         density,
-        (2, 512),
+        (2, 768),
         last=True,
     )
 

time: 82.5 us -> 82.7 us (level)
    pallas_call x7, Pallas kernels: 27.6 us -> 28.5 us  [add_terms(): pl.pallas_call(functools.partial(terms_kernel, pieces, mode, shape), out_...]
  transfers between devices with their start and end apart: 17 -> 17, of which waited for: 7 -> 7; matrix products, arithmetic and copies ran while one was open for 1% -> 1% of each run, Pallas kernels for 25% -> 26%
where the time goes in v1:
time: 82.7 us; the launch traced here: 82.1 us
  Pallas kernels  28.6 us (35%)
  starting transfers between devices  24.2 us (29%)
  waiting for transfers between devices  24.1 us (29%)
  local copies, waits for them, and re-layouts  2.7 us (3%)
  matrix products  1.75 us (2%)
    pallas_call x7, Pallas kernels, add_terms(): pl.pallas_call(functools.partial(terms_kernel, pieces, mode, shape), out_...  28.5 us
    all_to_all x1, waiting for transfers between devices, to_owner(): lax.all_to_all(columns, 'wide', split_axis=1, concat_axis=0, tiled=True)  18.4 us
    ppermute x9, starting transfers between devices, swap_by(): return lax.ppermute(shard, axis, [(i, i ^ bit) for i in range(peers)])  7.48 us
    all_to_all x1, starting transfers between devices, to_owner(): lax.all_to_all(columns, 'wide', split_axis=1, concat_axis=0, tiled=True)  7.35 us
    ppermute x3, starting transfers between devices, hand_along(): lax.ppermute(shard, axis, [(i, (i + (4 if i // 2 % 2 == 0 else -4)) % pee...  5.4 us
    ppermute x4, starting transfers between devices, from_behind(): lax.ppermute(shard, axis, [(i, (i + by) % peers) for i in range(peers)])  3.96 us
    ppermute x4, waiting for transfers between devices, from_behind(): lax.ppermute(shard, axis, [(i, (i + by) % peers) for i in range(peers)])  2.97 us
    ppermute x9, waiting for transfers between devices, swap_by(): return lax.ppermute(shard, axis, [(i, i ^ bit) for i in range(peers)])  2.5 us
  transfers between devices with their start and end apart: 17, of which 7 were waited for; matrix products, arithmetic and copies ran while one was open for 1% of the time, Pallas kernels for 26%

profile of v1, /device:TPU:1, one launch (start us, length us, event | category | flops | bytes accessed | tf_op | source)
XLA Modules:
  0.0 82.1 jit_solution(1454918663518937099)
XLA Ops:
  0.0 0.0 copy-start
  0.0 1.5 %copy-done = bf16[96,16,640]{2,1,0:T(8,128)(2,1)S(1)} copy-done((bf16[96,16,640]{2,1,0:T(8,128)(2,1)S(1)}, bf16[96,16,640]{2,1,0:T(8,128)(2,1)}, u32[]{:S(2)}) %copy-start) | copy-done | bytes 1966104
  1.5 1.7 %convolution_convert_fusion = bf16[1536,256]{1,0:T(8,128)(2,1)S(1)} fusion(bf16[1536,640]{1,0:T(8,128)(2,1)S(1)} %bitcast.11, bf16[640,256]{1,0:T(8,128)(2,1)} %param.6), kind=kOutput, calls=%fused_computation | convolution fusion | flops 503709696 | bytes 3080192 | tf_op jit(solution)/shard_map/dot_general | solution.py:232
  3.3 0.0 copy-start.1
  3.3 0.0 copy-start.2
  3.3 0.0 copy-start.3
  3.3 1.1 %copy.11 = bf16[96,16,256]{2,0,1:T(8,128)(2,1)} copy(bf16[96,16,256]{2,1,0:T(8,128)(2,1)S(1)} %bitcast.14) | data formatting | bytes 1572864 | tf_op jit(solution)/shard_map/reshape | solution.py:237
  4.5 7.4 %all-to-all-start = ((bf16[96,16,256]{2,0,1:T(8,128)(2,1)}), bf16[96,16,256]{2,0,1:T(8,128)(2,1)S(1)}, u32[]{:S(2)}, u32[]{:S(2)}) async-start(bf16[96,16,256]{2,0,1:T(8,128)(2,1)} %copy.11), calls=%async_computation | async-start | bytes 1572864 | tf_op jit(solution)/shard_map/all_to_all | solution.py:214
  11.8 0.0 copy-done.1
  11.8 0.0 copy-done.2
  11.8 0.0 copy-done.3
  11.9 0.1 pad_maximum_fusion.1.refs_1_
  11.9 0.1 pad_add_fusion.refs_0_
  12.0 18.4 %all-to-all-done = bf16[96,16,256]{2,0,1:T(8,128)(2,1)S(1)} async-done(((bf16[96,16,256]{2,0,1:T(8,128)(2,1)}), bf16[96,16,256]{2,0,1:T(8,128)(2,1)S(1)}, u32[]{:S(2)}, u32[]{:S(2)}) %all-to-all-start) | async-done | bytes 786464 | tf_op jit(solution)/shard_map/all_to_all | solution.py:214
  30.4 0.3 collective-permute-start.3
  30.6 0.1 shard_map.55
  30.8 1.1 %collective-permute-start.1 = (bf16[1536,128]{1,0:T(8,128)(2,1)S(1)}, bf16[1536,128]{1,0:T(8,128)(2,1)S(1)}, u32[]{:S(2)}, u32[]{:S(2)}) collective-permute-start(bf16[1536,128]{1,0:T(8,128)(2,1)S(1)} %get-tuple-element.52.refs_3_), channel_id=1, source_target_pairs={{0,4},{2,6},{4,0},{6,2},{8,12},{10,14},{12,8},{14,10},{16,20},{18,... | collective-permute-start | bytes 1179656 | tf_op jit(solution)/shard_map/ppermute | solution.py:23
  31.9 1.2 %collective-permute-start.2 = (bf16[1536,128]{1,0:T(8,128)(2,1)S(1)}, bf16[1536,128]{1,0:T(8,128)(2,1)S(1)}, u32[]{:S(2)}, u32[]{:S(2)}) collective-permute-start(bf16[1536,128]{1,0:T(8,128)(2,1)S(1)} %get-tuple-element.56.refs_4_), channel_id=1, source_target_pairs={{0,1},{1,0},{2,3},{3,2},{4,5},{5,4},{6,7},{7,6},{8,9},{9,8},{10,11... | collective-permute-start | bytes 1179656 | tf_op jit(solution)/shard_map/ppermute | solution.py:18
  33.1 3.3 %shard_map.56 = (bf16[256,1536]{1,0:T(8,128)(2,1)S(1)}, f32[256,128]{1,0:T(8,128)S(1)}, f32[8,256,128]{2,1,0:T(8,128)S(1)}, f32[10,256]{1,0:T(8,128)S(1)}, f32[8...) custom-call(s32[3]{0:T(128)S(1)} %pad_add_fusion.refs_0_, f32[24]{0:T(128)S(1)} %pad_maximum_fusion.1.refs_1_, ...), custom_call_target="tpu_custom_call" | custom-call | flops 1 | bytes 1 | tf_op jit(solution)/shard_map/pallas_call | solution.py:192
  36.5 0.3 collective-permute-start
  36.8 0.4 collective-permute-start.4
  37.2 0.0 collective-permute-done.3.refs_5_
  37.2 3.4 %shard_map.57.refs_7_ = f32[8,256,1536]{2,1,0:T(8,128)S(1)} custom-call(bf16[256,1536]{1,0:T(8,128)(2,1)S(1)} %get-tuple-element.45.refs_0_, f32[256,128]{1,0:T(8,128)S(1)} %get-tuple-element.46.refs_1_, f32[8,256,128]{2,1,0:T(8,128)S(1)} %get-tuple-element.47.refs_2_, f32[10,256]{1,0:T(8,128)S(1)} %get-tuple-element.48.refs_3_, ...), custom_call_target="tpu_custom_call", output_to_operand_aliasing={{}: (6, {})} | custom-call | flops 1 | bytes 1 | tf_op jit(solution)/shard_map/pallas_call | solution.py:192
  40.6 0.7 collective-permute-done.1.refs_6_
  41.3 0.5 collective-permute-done.2.refs_5_
  41.8 0.7 collective-permute-start.5
  42.4 2.0 %collective-permute-start.6 = (bf16[1536,128]{1,0:T(8,128)(2,1)S(1)}, bf16[1536,128]{1,0:T(8,128)(2,1)S(1)}, u32[]{:S(2)}, u32[]{:S(2)}) collective-permute-start(bf16[1536,128]{1,0:T(8,128)(2,1)S(1)} %collective-permute-done.1.refs_6_), channel_id=1, source_target_pairs={{0,8},{2,10},{4,28},{6,30},{8,16},{10,18},{12,4},{14,6},{16,24},{1... | collective-permute-start | bytes 1179656 | tf_op jit(solution)/shard_map/ppermute | solution.py:28
  44.5 3.2 %shard_map.58.refs_7_ = f32[8,256,1536]{2,1,0:T(8,128)S(1)} custom-call(bf16[256,1536]{1,0:T(8,128)(2,1)S(1)} %get-tuple-element.45.refs_0_, f32[256,128]{1,0:T(8,128)S(1)} %get-tuple-element.46.refs_1_, f32[8,256,128]{2,1,0:T(8,128)S(1)} %get-tuple-element.47.refs_2_, f32[10,256]{1,0:T(8,128)S(1)} %get-tuple-element.48.refs_3_, ...), custom_call_target="tpu_custom_call", output_to_operand_aliasing={{}: (7, {})} | custom-call | flops 1 | bytes 1 | tf_op jit(solution)/shard_map/pallas_call | solution.py:192
  47.7 2.5 %collective-permute-done.refs_5_ = bf16[1536,128]{1,0:T(8,128)(2,1)S(1)} collective-permute-done((bf16[1536,128]{1,0:T(8,128)(2,1)S(1)}, bf16[1536,128]{1,0:T(8,128)(2,1)S(1)}, u32[]{:S(2)}, u32[]{:S(2)}) %collective-permute-start) | collective-permute-done | bytes 393248 | tf_op jit(solution)/shard_map/ppermute | solution.py:18
  50.2 0.0 collective-permute-done.4.refs_6_
  50.2 2.4 %collective-permute-start.7 = (bf16[1536,128]{1,0:T(8,128)(2,1)S(1)}, bf16[1536,128]{1,0:T(8,128)(2,1)S(1)}, u32[]{:S(2)}, u32[]{:S(2)}) collective-permute-start(bf16[1536,128]{1,0:T(8,128)(2,1)S(1)} %collective-permute-done.4.refs_6_), channel_id=1, source_target_pairs={{0,8},{2,10},{4,28},{6,30},{8,16},{10,18},{12,4},{14,6},{16,24},{1... | collective-permute-start | bytes 1179656 | tf_op jit(solution)/shard_map/ppermute | solution.py:28
  52.6 1.2 %collective-permute-start.8 = (bf16[1536,128]{1,0:T(8,128)(2,1)S(1)}, bf16[1536,128]{1,0:T(8,128)(2,1)S(1)}, u32[]{:S(2)}, u32[]{:S(2)}) collective-permute-start(bf16[1536,128]{1,0:T(8,128)(2,1)S(1)} %collective-permute-done.1.refs_6_), channel_id=1, source_target_pairs={{0,1},{1,0},{2,3},{3,2},{4,5},{5,4},{6,7},{7,6},{8,9},{9,8},{10,11... | collective-permute-start | bytes 1179656 | tf_op jit(solution)/shard_map/ppermute | solution.py:18
  53.8 0.1 pad_maximum_fusion
  53.9 2.1 %collective-permute-start.13 = (bf16[1536,256]{1,0:T(8,128)(2,1)S(1)}, bf16[1536,256]{1,0:T(8,128)(2,1)S(1)}, u32[]{:S(2)}, u32[]{:S(2)}) collective-permute-start(bf16[1536,256]{1,0:T(8,128)(2,1)S(1)} %pad_maximum_fusion), channel_id=1, source_target_pairs={{0,2},{2,0},{4,6},{6,4},{8,10},{10,8},{12,14},{14,12},{16,18},{18,... | collective-permute-start | bytes 2359304 | tf_op jit(solution)/shard_map/ppermute | solution.py:23
  55.9 3.0 %shard_map.59.refs_7_ = f32[8,256,1536]{2,1,0:T(8,128)S(1)} custom-call(bf16[256,1536]{1,0:T(8,128)(2,1)S(1)} %get-tuple-element.45.refs_0_, f32[256,128]{1,0:T(8,128)S(1)} %get-tuple-element.46.refs_1_, f32[8,256,128]{2,1,0:T(8,128)S(1)} %get-tuple-element.47.refs_2_, f32[10,256]{1,0:T(8,128)S(1)} %get-tuple-element.48.refs_3_, ...), custom_call_target="tpu_custom_call", output_to_operand_aliasing={{}: (7, {})} | custom-call | flops 1 | bytes 1 | tf_op jit(solution)/shard_map/pallas_call | solution.py:192
  59.0 0.0 collective-permute-done.5.refs_6_
  59.0 0.0 collective-permute-done.6.refs_5_
  59.0 1.0 %collective-permute-start.11 = (bf16[1536,128]{1,0:T(8,128)(2,1)S(1)}, bf16[1536,128]{1,0:T(8,128)(2,1)S(1)}, u32[]{:S(2)}, u32[]{:S(2)}) collective-permute-start(bf16[1536,128]{1,0:T(8,128)(2,1)S(1)} %collective-permute-done.5.refs_6_), channel_id=1, source_target_pairs={{0,8},{2,10},{4,28},{6,30},{8,16},{10,18},{12,4},{14,6},{16,24},{1... | collective-permute-start | bytes 1179656 | tf_op jit(solution)/shard_map/ppermute | solution.py:28
  60.0 1.2 %collective-permute-start.12 = (bf16[1536,128]{1,0:T(8,128)(2,1)S(1)}, bf16[1536,128]{1,0:T(8,128)(2,1)S(1)}, u32[]{:S(2)}, u32[]{:S(2)}) collective-permute-start(bf16[1536,128]{1,0:T(8,128)(2,1)S(1)} %collective-permute-done.6.refs_5_), channel_id=1, source_target_pairs={{0,1},{1,0},{2,3},{3,2},{4,5},{5,4},{6,7},{7,6},{8,9},{9,8},{10,11... | collective-permute-start | bytes 1179656 | tf_op jit(solution)/shard_map/ppermute | solution.py:18
  61.2 3.0 %shard_map.60.refs_8_ = f32[8,256,1536]{2,1,0:T(8,128)S(1)} custom-call(bf16[256,1536]{1,0:T(8,128)(2,1)S(1)} %get-tuple-element.45.refs_0_, f32[256,128]{1,0:T(8,128)S(1)} %get-tuple-element.46.refs_1_, f32[8,256,128]{2,1,0:T(8,128)S(1)} %get-tuple-element.47.refs_2_, f32[10,256]{1,0:T(8,128)S(1)} %get-tuple-element.48.refs_3_, ...), custom_call_target="tpu_custom_call", output_to_operand_aliasing={{}: (7, {})} | custom-call | flops 1 | bytes 1 | tf_op jit(solution)/shard_map/pallas_call | solution.py:192
  64.2 0.0 collective-permute-done.7.refs_6_
  64.2 0.0 collective-permute-done.8.refs_5_
  64.3 2.0 %collective-permute-start.10 = (bf16[1536,128]{1,0:T(8,128)(2,1)S(1)}, bf16[1536,128]{1,0:T(8,128)(2,1)S(1)}, u32[]{:S(2)}, u32[]{:S(2)}) collective-permute-start(bf16[1536,128]{1,0:T(8,128)(2,1)S(1)} %broadcast_select_fusion.2), channel_id=1, source_target_pairs={{0,2},{2,0},{4,6},{6,4},{8,10},{10,8},{12,14},{14,12},{16,18},{18,... | collective-permute-start | bytes 1179656 | tf_op jit(solution)/shard_map/ppermute | solution.py:23
  66.3 0.1 collective-permute-start.9
  66.4 0.0 collective-permute-done.13.refs_7_
  66.4 5.1 %shard_map.61.refs_11_ = f32[8,256,1536]{2,1,0:T(8,128)S(1)} custom-call(bf16[256,1536]{1,0:T(8,128)(2,1)S(1)} %get-tuple-element.45.refs_0_, f32[256,128]{1,0:T(8,128)S(1)} %get-tuple-element.46.refs_1_, f32[8,256,128]{2,1,0:T(8,128)S(1)} %get-tuple-element.47.refs_2_, f32[10,256]{1,0:T(8,128)S(1)} %get-tuple-element.48.refs_3_, ...), custom_call_target="tpu_custom_call", output_to_operand_aliasing={{}: (8, {})} | custom-call | flops 1 | bytes 1 | tf_op jit(solution)/shard_map/pallas_call | solution.py:192
  71.6 0.3 collective-permute-done.11.refs_8_
  71.9 0.0 collective-permute-done.12.refs_7_
  71.9 0.8 collective-permute-start.15
  72.8 0.1 collective-permute-start.14
  72.9 0.0 collective-permute-done.10.refs_6_
  72.9 0.0 collective-permute-done.9.refs_5_
  72.9 1.2 %collective-permute-done.15.refs_10_ = bf16[1536,128]{1,0:T(8,128)(2,1)S(1)} collective-permute-done((bf16[1536,128]{1,0:T(8,128)(2,1)S(1)}, bf16[1536,128]{1,0:T(8,128)(2,1)S(1)}, u32[]{:S(2)}, u32[]{:S(2)}) %collective-permute-start.15) | collective-permute-done | bytes 393248 | tf_op jit(solution)/shard_map/ppermute | solution.py:23
  74.1 0.6 collective-permute-done.14.refs_9_
  74.6 7.3 %shard_map.62 = bf16[8,1,256,1536]{3,2,1,0:T(8,128)(2,1)} custom-call(bf16[256,1536]{1,0:T(8,128)(2,1)S(1)} %get-tuple-element.45.refs_0_, f32[256,128]{1,0:T(8,128)S(1)} %get-tuple-element.46.refs_1_, f32[8,256,128]{2,1,0:T(8,128)S(1)} %get-tuple-element.47.refs_2_, f32[10,256]{1,0:T(8,128)S(1)} %get-tuple-element.48.refs_3_, ...), custom_call_target="tpu_custom_call" | custom-call | flops 1 | bytes 1 | tf_op jit(solution)/shard_map/pallas_call | solution.py:192
  (5 shorter events, 0.2 us)
Async XLA Ops:
  0.0 1.5 %copy-start = (bf16[96,16,640]{2,1,0:T(8,128)(2,1)S(1)}, bf16[96,16,640]{2,1,0:T(8,128)(2,1)}, u32[]{:S(2)}) copy-start(bf16[96,16,640]{2,1,0:T(8,128)(2,1)} %param.5) | copy-start | bytes 5898244
  3.3 8.5 %copy-start.1 = (f32[512]{0:T(512)S(1)}, f32[512]{0:T(512)}, u32[]{:S(2)}) copy-start(f32[512]{0:T(512)} %param.8) | copy-start | bytes 6148
  3.3 8.5 %copy-start.2 = (f32[16]{0:T(128)S(1)}, f32[16]{0:T(128)}, u32[]{:S(2)}) copy-start(f32[16]{0:T(128)} %param.7) | copy-start | bytes 196
  3.3 8.5 %copy-start.3 = (f32[8]{0:T(128)S(1)}, f32[8]{0:T(128)}, u32[]{:S(2)}) copy-start(f32[8]{0:T(128)} %param.9) | copy-start | bytes 100
  4.5 25.9 %all-to-all-start = ((bf16[96,16,256]{2,0,1:T(8,128)(2,1)}), bf16[96,16,256]{2,0,1:T(8,128)(2,1)S(1)}, u32[]{:S(2)}, u32[]{:S(2)}) async-start(bf16[96,16,256]{2,0,1:T(8,128)(2,1)} %copy.11), calls=%async_computation | async-start | bytes 1572864 | tf_op jit(solution)/shard_map/all_to_all | solution.py:214
  30.4 6.8 %collective-permute-start.3 = (bf16[1536,256]{1,0:T(8,128)(2,1)S(1)}, bf16[1536,256]{1,0:T(8,128)(2,1)S(1)}, u32[]{:S(2)}, u32[]{:S(2)}) collective-permute-start(bf16[1536,256]{1,0:T(8,128)(2,1)S(1)} %bitcast.12), channel_id=1, source_target_pairs={{0,2},{2,0},{4,6},{6,4},{8,10},{10,8},{12,14},{14,12},{16,18},{18,... | collective-permute-start | bytes 2359304 | tf_op jit(solution)/shard_map/ppermute | solution.py:23
  30.8 10.5 %collective-permute-start.1 = (bf16[1536,128]{1,0:T(8,128)(2,1)S(1)}, bf16[1536,128]{1,0:T(8,128)(2,1)S(1)}, u32[]{:S(2)}, u32[]{:S(2)}) collective-permute-start(bf16[1536,128]{1,0:T(8,128)(2,1)S(1)} %get-tuple-element.52.refs_3_), channel_id=1, source_target_pairs={{0,4},{2,6},{4,0},{6,2},{8,12},{10,14},{12,8},{14,10},{16,20},{18,... | collective-permute-start | bytes 1179656 | tf_op jit(solution)/shard_map/ppermute | solution.py:23
  31.9 9.9 %collective-permute-start.2 = (bf16[1536,128]{1,0:T(8,128)(2,1)S(1)}, bf16[1536,128]{1,0:T(8,128)(2,1)S(1)}, u32[]{:S(2)}, u32[]{:S(2)}) collective-permute-start(bf16[1536,128]{1,0:T(8,128)(2,1)S(1)} %get-tuple-element.56.refs_4_), channel_id=1, source_target_pairs={{0,1},{1,0},{2,3},{3,2},{4,5},{5,4},{6,7},{7,6},{8,9},{9,8},{10,11... | collective-permute-start | bytes 1179656 | tf_op jit(solution)/shard_map/ppermute | solution.py:18
  36.5 13.7 %collective-permute-start = (bf16[1536,128]{1,0:T(8,128)(2,1)S(1)}, bf16[1536,128]{1,0:T(8,128)(2,1)S(1)}, u32[]{:S(2)}, u32[]{:S(2)}) collective-permute-start(bf16[1536,128]{1,0:T(8,128)(2,1)S(1)} %get-tuple-element.52.refs_3_), channel_id=1, source_target_pairs={{0,1},{1,0},{2,3},{3,2},{4,5},{5,4},{6,7},{7,6},{8,9},{9,8},{10,11... | collective-permute-start | bytes 1179656 | tf_op jit(solution)/shard_map/ppermute | solution.py:18
  36.8 13.4 %collective-permute-start.4 = (bf16[1536,128]{1,0:T(8,128)(2,1)S(1)}, bf16[1536,128]{1,0:T(8,128)(2,1)S(1)}, u32[]{:S(2)}, u32[]{:S(2)}) collective-permute-start(bf16[1536,128]{1,0:T(8,128)(2,1)S(1)} %get-tuple-element.56.refs_4_), channel_id=1, source_target_pairs={{0,4},{2,6},{4,0},{6,2},{8,12},{10,14},{12,8},{14,10},{16,20},{18,... | collective-permute-start | bytes 1179656 | tf_op jit(solution)/shard_map/ppermute | solution.py:23
  41.8 17.2 %collective-permute-start.5 = (bf16[1536,128]{1,0:T(8,128)(2,1)S(1)}, bf16[1536,128]{1,0:T(8,128)(2,1)S(1)}, u32[]{:S(2)}, u32[]{:S(2)}) collective-permute-start(bf16[1536,128]{1,0:T(8,128)(2,1)S(1)} %collective-permute-done.2.refs_5_), channel_id=1, source_target_pairs={{0,4},{2,6},{4,0},{6,2},{8,12},{10,14},{12,8},{14,10},{16,20},{18,... | collective-permute-start | bytes 1179656 | tf_op jit(solution)/shard_map/ppermute | solution.py:23
  42.4 16.5 %collective-permute-start.6 = (bf16[1536,128]{1,0:T(8,128)(2,1)S(1)}, bf16[1536,128]{1,0:T(8,128)(2,1)S(1)}, u32[]{:S(2)}, u32[]{:S(2)}) collective-permute-start(bf16[1536,128]{1,0:T(8,128)(2,1)S(1)} %collective-permute-done.1.refs_6_), channel_id=1, source_target_pairs={{0,8},{2,10},{4,28},{6,30},{8,16},{10,18},{12,4},{14,6},{16,24},{1... | collective-permute-start | bytes 1179656 | tf_op jit(solution)/shard_map/ppermute | solution.py:28
  50.2 14.0 %collective-permute-start.7 = (bf16[1536,128]{1,0:T(8,128)(2,1)S(1)}, bf16[1536,128]{1,0:T(8,128)(2,1)S(1)}, u32[]{:S(2)}, u32[]{:S(2)}) collective-permute-start(bf16[1536,128]{1,0:T(8,128)(2,1)S(1)} %collective-permute-done.4.refs_6_), channel_id=1, source_target_pairs={{0,8},{2,10},{4,28},{6,30},{8,16},{10,18},{12,4},{14,6},{16,24},{1... | collective-permute-start | bytes 1179656 | tf_op jit(solution)/shard_map/ppermute | solution.py:28
  52.6 11.7 %collective-permute-start.8 = (bf16[1536,128]{1,0:T(8,128)(2,1)S(1)}, bf16[1536,128]{1,0:T(8,128)(2,1)S(1)}, u32[]{:S(2)}, u32[]{:S(2)}) collective-permute-start(bf16[1536,128]{1,0:T(8,128)(2,1)S(1)} %collective-permute-done.1.refs_6_), channel_id=1, source_target_pairs={{0,1},{1,0},{2,3},{3,2},{4,5},{5,4},{6,7},{7,6},{8,9},{9,8},{10,11... | collective-permute-start | bytes 1179656 | tf_op jit(solution)/shard_map/ppermute | solution.py:18
  53.9 12.6 %collective-permute-start.13 = (bf16[1536,256]{1,0:T(8,128)(2,1)S(1)}, bf16[1536,256]{1,0:T(8,128)(2,1)S(1)}, u32[]{:S(2)}, u32[]{:S(2)}) collective-permute-start(bf16[1536,256]{1,0:T(8,128)(2,1)S(1)} %pad_maximum_fusion), channel_id=1, source_target_pairs={{0,2},{2,0},{4,6},{6,4},{8,10},{10,8},{12,14},{14,12},{16,18},{18,... | collective-permute-start | bytes 2359304 | tf_op jit(solution)/shard_map/ppermute | solution.py:23
  59.0 12.9 %collective-permute-start.11 = (bf16[1536,128]{1,0:T(8,128)(2,1)S(1)}, bf16[1536,128]{1,0:T(8,128)(2,1)S(1)}, u32[]{:S(2)}, u32[]{:S(2)}) collective-permute-start(bf16[1536,128]{1,0:T(8,128)(2,1)S(1)} %collective-permute-done.5.refs_6_), channel_id=1, source_target_pairs={{0,8},{2,10},{4,28},{6,30},{8,16},{10,18},{12,4},{14,6},{16,24},{1... | collective-permute-start | bytes 1179656 | tf_op jit(solution)/shard_map/ppermute | solution.py:28
  60.0 11.9 %collective-permute-start.12 = (bf16[1536,128]{1,0:T(8,128)(2,1)S(1)}, bf16[1536,128]{1,0:T(8,128)(2,1)S(1)}, u32[]{:S(2)}, u32[]{:S(2)}) collective-permute-start(bf16[1536,128]{1,0:T(8,128)(2,1)S(1)} %collective-permute-done.6.refs_5_), channel_id=1, source_target_pairs={{0,1},{1,0},{2,3},{3,2},{4,5},{5,4},{6,7},{7,6},{8,9},{9,8},{10,11... | collective-permute-start | bytes 1179656 | tf_op jit(solution)/shard_map/ppermute | solution.py:18
  64.3 8.6 %collective-permute-start.10 = (bf16[1536,128]{1,0:T(8,128)(2,1)S(1)}, bf16[1536,128]{1,0:T(8,128)(2,1)S(1)}, u32[]{:S(2)}, u32[]{:S(2)}) collective-permute-start(bf16[1536,128]{1,0:T(8,128)(2,1)S(1)} %broadcast_select_fusion.2), channel_id=1, source_target_pairs={{0,2},{2,0},{4,6},{6,4},{8,10},{10,8},{12,14},{14,12},{16,18},{18,... | collective-permute-start | bytes 1179656 | tf_op jit(solution)/shard_map/ppermute | solution.py:23
  66.3 6.5 %collective-permute-start.9 = (bf16[1536,128]{1,0:T(8,128)(2,1)S(1)}, bf16[1536,128]{1,0:T(8,128)(2,1)S(1)}, u32[]{:S(2)}, u32[]{:S(2)}) collective-permute-start(bf16[1536,128]{1,0:T(8,128)(2,1)S(1)} %broadcast_select_fusion.3), channel_id=1, source_target_pairs={{0,2},{2,0},{4,6},{6,4},{8,10},{10,8},{12,14},{14,12},{16,18},{18,... | collective-permute-start | bytes 1179656 | tf_op jit(solution)/shard_map/ppermute | solution.py:23
  71.9 2.1 %collective-permute-start.15 = (bf16[1536,128]{1,0:T(8,128)(2,1)S(1)}, bf16[1536,128]{1,0:T(8,128)(2,1)S(1)}, u32[]{:S(2)}, u32[]{:S(2)}) collective-permute-start(bf16[1536,128]{1,0:T(8,128)(2,1)S(1)} %broadcast_select_fusion), channel_id=1, source_target_pairs={{0,2},{2,0},{4,6},{6,4},{8,10},{10,8},{12,14},{14,12},{16,18},{18,... | collective-permute-start | bytes 1179656 | tf_op jit(solution)/shard_map/ppermute | solution.py:23
  72.8 1.9 %collective-permute-start.14 = (bf16[1536,128]{1,0:T(8,128)(2,1)S(1)}, bf16[1536,128]{1,0:T(8,128)(2,1)S(1)}, u32[]{:S(2)}, u32[]{:S(2)}) collective-permute-start(bf16[1536,128]{1,0:T(8,128)(2,1)S(1)} %broadcast_select_fusion.1), channel_id=1, source_target_pairs={{0,2},{2,0},{4,6},{6,4},{8,10},{10,8},{12,14},{14,12},{16,18},{18,... | collective-permute-start | bytes 1179656 | tf_op jit(solution)/shard_map/ppermute | solution.py:23
